TPU v7x, 512 devices: a whole 4x4x16 slice. The times are simulated.
512 devices in a mesh: group: 4 (over z_hi), dp: 32 (over y, z_lo, core), tensor: 4 (over x).
Axes of the slice: x: 4, y: 4, z: 16 (z_hi: 4, z_lo: 4; z = z_hi * 4 + z_lo), core: 2. Of those that a mesh axis runs over, the one named last changes fastest.
Arguments:
- queries: bfloat16 [16384, 4096], P(('group', 'dp'), 'tensor'), may hold values from -16 to 16
- span_state: bfloat16 [16384, 4096], P(('group', 'dp'), 'tensor'), may hold values from -6 to 6
- neigh_state: bfloat16 [65536, 4096], P(('group', 'dp'), 'tensor'), may hold values from -24 to 24
- counts: int32 [4, 64], P('group'), may hold values from 1 to 2
- norm_gain: float32 [4096], P('tensor'), may hold values from 0.5 to 1.5
- head_gate: float32 [32], P('tensor'), may hold values from 0.3 to 1.5
- out_grad: bfloat16 [16384, 4096], P(('group', 'dp'), 'tensor'), may hold values from -6 to 6
Outputs:
- cross_output: bfloat16 [16384, 4096], P(('group', 'dp'), 'tensor')
- query_grad: bfloat16 [16384, 4096], P(('group', 'dp'), 'tensor')
- span_grad: bfloat16 [16384, 4096], P(('group', 'dp'), 'tensor')
- neighbour_grad: bfloat16 [65536, 4096], P(('group', 'dp'), 'tensor')
- gate_grad: float32 [32], P('tensor')
Inputs may be any that keep to these rules, and one draw needn't show every extreme that they name: Slot j of span c holds a retrieved neighbour exactly when j < counts[c].
All inputs are finite; a program needn't handle non-finite values.
Results may differ from a plain program's by a relative error of at most 0.0095.
The roundings to bfloat16 on the way count: a program that leaves them out, or rounds other values in their place, can miss the bound.
Values may be sent and summed in bfloat16 or wider, within the bound.
No kernel may reach another device: no remote copies, remote signals or barrier semaphores. Data moves between devices by JAX's collectives and lax.ppermute only.
A program may use at most 64 MiB of HBM per device.

v0:
```python
import math
import jax
import jax.numpy as jnp
from jax import lax
from jax.sharding import PartitionSpec as P

CH = 64
NB = 2
NL = 128
epsilon = 1e-05
masked_score = -1e30


def shifted(value, axis, steps):
    count = lax.axis_size(axis)
    leading, last = (max(0, -steps), min(count, count - steps))
    return lax.ppermute(value, axis, [(source, source + steps) for source in range(leading, last)])


def product(form, left, right):
    return jnp.einsum(form, left, right, preferred_element_type=jnp.float32)


def encoder_forward(normed, neighbours, contexts):
    slot_count = normed.shape[1]
    spread = jnp.broadcast_to(
        contexts[:, None], (contexts.shape[0], slot_count) + contexts.shape[1:]
    )
    all_keys = jnp.concatenate([normed, spread], axis=2)
    scores = product("cjqhd,cjkhd->cjhqk", normed, all_keys) / normed.shape[-1]
    powers = jnp.exp(scores)
    weights = powers / jnp.sum(powers, axis=-1, keepdims=True)
    rounded = weights.astype(jnp.bfloat16)
    mixture = product("cjhqk,cjkhd->cjqhd", rounded, all_keys)
    encoded = (neighbours.astype(jnp.float32) + mixture).astype(jnp.bfloat16)
    return (encoded, (all_keys, weights, rounded, mixture))


def encoder_backward(grad_encoded, normed, saved):
    all_keys, weights, rounded, mixture = saved
    grad_rounded = grad_encoded.astype(jnp.bfloat16)
    grad_weights = product("cjqhd,cjkhd->cjhqk", grad_rounded, all_keys)
    offset = jnp.moveaxis(jnp.sum(grad_encoded * mixture, axis=-1), -1, 2)[..., None]
    score_grad = (weights * (grad_weights - offset) / normed.shape[-1]).astype(jnp.bfloat16)
    normed_grad = product("cjhqk,cjkhd->cjqhd", score_grad, all_keys)
    key_grad = product("cjhqk,cjqhd->cjkhd", score_grad, normed) + product(
        "cjhqk,cjqhd->cjkhd", rounded, grad_rounded
    )
    length = normed.shape[2]
    normed_grad = normed_grad + key_grad[:, :, :length]
    context_grad = jnp.sum(key_grad[:, :, length:], axis=1)
    return (normed_grad, context_grad)


def cross_attend(blocks, grad_blocks, keys, usable, present, gate_tanh):
    scale = 1.0 / math.sqrt(blocks.shape[-1])
    scores = product("brhd,bmhd->bhrm", blocks, keys) * scale
    scores = jnp.where(usable[:, None, None, :], scores, masked_score)
    highest = jnp.max(scores, axis=-1, keepdims=True)
    powers = jnp.exp(scores - highest)
    weights = powers / jnp.sum(powers, axis=-1, keepdims=True)
    rounded = weights.astype(jnp.bfloat16)
    attended = product("bhrm,bmhd->brhd", rounded, keys)
    present_mask = present[:, None, None, None]
    attended = jnp.where(present_mask, attended, 0.0)
    output = (gate_tanh[:, None] * attended).astype(jnp.bfloat16)
    grad_output = grad_blocks.astype(jnp.float32)
    gate_term = jnp.sum(grad_output * attended, axis=(0, 1, 3))
    att_grad = jnp.where(present_mask, gate_tanh[:, None] * grad_output, 0.0)
    grad_rounded = att_grad.astype(jnp.bfloat16)
    grad_weights = product("brhd,bmhd->bhrm", grad_rounded, keys)
    offset = jnp.moveaxis(jnp.sum(att_grad * attended, axis=-1), -1, 1)[..., None]
    score_grad = (weights * (grad_weights - offset) * scale).astype(jnp.bfloat16)
    query_grad = product("bhrm,bmhd->brhd", score_grad, keys).astype(jnp.bfloat16)
    key_grad = product("bhrm,brhd->bmhd", score_grad, blocks) + product(
        "bhrm,brhd->bmhd", rounded, grad_rounded
    )
    return (output, query_grad, key_grad, gate_term)


def shards(queries, span_state, neigh_state, counts, norm_gain, head_gate, out_grad):
    head_count = head_gate.shape[0]
    local_width = queries.shape[1]
    head_dim = local_width // head_count
    row_count = queries.shape[0]
    span_count = row_count // CH
    seq_spans = counts.shape[1]
    lead = CH - 1

    def blockify(matrix):
        return matrix.reshape(-1, CH, head_count, head_dim)

    neighbours = neigh_state.reshape(span_count, NB, NL, head_count, head_dim)
    contexts = span_state.reshape(span_count, CH, head_count, head_dim)
    gains = norm_gain.reshape(head_count, head_dim)
    floats = neighbours.astype(jnp.float32)
    square_sum = lax.psum(jnp.sum(floats * floats, axis=(3, 4)), "tensor")
    full_width = lax.axis_size("tensor") * local_width
    inverse = lax.rsqrt(square_sum / full_width + epsilon)[..., None, None]
    scaled = floats * inverse
    normed = (scaled * gains).astype(jnp.bfloat16)
    encoded, saved = encoder_forward(normed, neighbours, contexts)
    line_index = lax.axis_index("dp")
    first_span = line_index * span_count
    flat_counts = counts.reshape(-1)
    own_counts = lax.dynamic_slice_in_dim(flat_counts, first_span, span_count)
    gate_tanh = jnp.tanh(head_gate)
    usable = jnp.repeat(jnp.arange(NB)[None, :] < own_counts[:, None], NL, axis=1)
    present = own_counts > 0
    keys = encoded.reshape(span_count, NB * NL, head_count, head_dim)
    kept = row_count - lead
    padding = jnp.zeros((lead, local_width), jnp.bfloat16)
    blocks = blockify(jnp.concatenate([queries[lead:], padding], axis=0))
    grad_blocks = blockify(jnp.concatenate([out_grad[lead:], padding], axis=0))
    earlier_keys = shifted(keys[span_count - 1], "dp", 1)
    earlier_count = lax.dynamic_index_in_dim(
        flat_counts, jnp.maximum(first_span - 1, 0), keepdims=False
    )
    earlier_present = jnp.logical_and(first_span % seq_spans > 0, earlier_count > 0)
    earlier_usable = jnp.repeat(jnp.arange(NB) < earlier_count, NL)
    front_row = jnp.zeros((1, local_width), jnp.bfloat16)
    first_block = blockify(jnp.concatenate([front_row, queries[:lead]], axis=0))
    first_grad = blockify(jnp.concatenate([front_row, out_grad[:lead]], axis=0))
    front_out, front_query, front_keys, front_term = cross_attend(
        first_block,
        first_grad,
        earlier_keys[None],
        earlier_usable[None],
        earlier_present[None],
        gate_tanh,
    )
    local_out, local_query, key_grad, local_term = cross_attend(
        blocks, grad_blocks, keys, usable, present, gate_tanh
    )
    returned = shifted(front_keys[0].astype(jnp.bfloat16), "dp", -1).astype(jnp.float32)
    key_grad = key_grad.at[span_count - 1].add(returned)
    cross_output = jnp.concatenate(
        [front_out.reshape(CH, local_width)[1:], local_out.reshape(row_count, local_width)[:kept]],
        axis=0,
    )
    query_grad = jnp.concatenate(
        [
            front_query.reshape(CH, local_width)[1:],
            local_query.reshape(row_count, local_width)[:kept],
        ],
        axis=0,
    )
    gate_terms = front_term + local_term
    grad_encoded = key_grad.reshape(span_count, NB, NL, head_count, head_dim)
    normed_grad, context_grad = encoder_backward(grad_encoded, normed, saved)
    gain_grad = normed_grad * gains
    projection = lax.psum(jnp.sum(gain_grad * scaled, axis=(3, 4)), "tensor") / full_width
    neighbour_grad = grad_encoded + inverse * (gain_grad - scaled * projection[..., None, None])
    total_tokens = lax.axis_size("group") * lax.axis_size("dp") * row_count
    summed = lax.psum(gate_terms, ("group", "dp"))
    gate_grad = (1.0 - gate_tanh * gate_tanh) * summed / math.sqrt(total_tokens)
    return (
        cross_output,
        query_grad,
        context_grad.reshape(row_count, local_width).astype(jnp.bfloat16),
        neighbour_grad.reshape(-1, local_width).astype(jnp.bfloat16),
        gate_grad,
    )


def solution(mesh):
    return jax.shard_map(
        shards,
        mesh=mesh,
        in_specs=(
            P(("group", "dp"), "tensor"),
            P(("group", "dp"), "tensor"),
            P(("group", "dp"), "tensor"),
            P("group", None),
            P("tensor"),
            P("tensor"),
            P(("group", "dp"), "tensor"),
        ),
        out_specs=(
            P(("group", "dp"), "tensor"),
            P(("group", "dp"), "tensor"),
            P(("group", "dp"), "tensor"),
            P(("group", "dp"), "tensor"),
            P("tensor"),
        ),
        check_vma=False,
    )
```

profile of v0, /device:TPU:2, one launch (start us, length us, event | category | flops | bytes accessed | tf_op | source)
XLA Modules:
  0.0 361.5 jit_solution(13486729681499176493)
XLA Ops:
  0.6 1.5 fusion.4
  2.2 2.8 convert_bitcast_fusion
  5.0 13.6 %psum.21 = f32[2,2,128]{2,1,0:T(2,128)S(1)} all-reduce(f32[2,2,128]{2,1,0:T(2,128)S(1)} %bitcast.184), channel_id=1, replica_groups=mesh['group'=4,'dp'=32,'tensor'=4] {'tensor'}, use_global_device_ids=true, to_apply=%region_1.0 | all-reduce | flops 512 | bytes 4096 | tf_op jit(solution)/shard_map/psum | solution.py:97
  18.7 2.1 copy.109
  21.5 0.8 fusion.3
  22.5 2.4 fusion.6
  25.0 0.9 copy-done.4
  26.3 0.9 copy.79
  27.2 2.1 collective-permute-start
  29.3 0.6 constant_dynamic-slice_fusion.1
  30.5 1.2 iota_compare_fusion.1
  31.8 0.7 slice.76
  32.5 1.9 copy.82
  35.0 0.6 broadcast_compare_fusion
  35.8 0.9 convert_bitcast_fusion.1
  36.8 0.9 copy.117
  38.2 1.0 copy-done.3
  39.2 1.2 fusion.66
  40.4 5.0 %multiply_reduce_fusion.1 = (f32[8]{0:T(128)}, f32[2,64,8]{1,2,0:T(8,128)}, bf16[2,64,8,128]{3,1,2,0:T(8,128)(2,1)}) fusion(f32[2,64,8,128]{3,2,1,0:T(8,128)} %bitcast.171, f32[8]{0:T(128)} %tanh.3, pred[2]{0:T(512)(128)(4,1)} %get-tuple-element.21, bf16[2,256,8,128]{3,2,1,0:T(8,128)(2,1)S(1)} %bitcast.155, f32[2,8,64]{2,1,0:T(8,128)S(1)} %get-tuple-element.30, ...), kind=kOutput, calls=%fused_computation.63 | convolution fusion | flops 69075192 | bytes 2891842 | tf_op jit(solution)/shard_map/bhrm,bmhd->brhd/dot_general | solution.py:21
  45.4 2.0 fusion.13
  47.4 1.0 fusion.26
  48.4 1.9 fusion.41
  50.3 0.8 convert_bitcast_fusion.3
  51.1 0.8 copy.115
  52.5 6.2 %add_bitcast_fusion.1 = f32[2,256,8,128]{1,3,2,0:T(8,128)} fusion(f32[2,8,128,256]{3,2,1,0:T(8,128)} %fusion.41, f32[2,64,8,128]{3,2,1,0:T(8,128)} %bitcast.173, f32[8]{0:T(128)S(1)} %copy-done.14, pred[2]{0:T(512)(128)(4,1)S(1)} %copy-done.16, f32[2,8,64]{2,1,0:T(8,128)S(1)} %get-tuple-element.30, f32[2,8,64,256]{3,2,1,0:T(8,128)} %copy-done.3), kind=kOutput, calls=%fused_computation.18 | convolution fusion | flops 68814080 | bytes 5771298 | tf_op jit(solution)/shard_map/bhrm,brhd->bmhd/dot_general | solution.py:21
  58.6 1.4 fusion.21
  60.0 0.9 fusion.67
  60.9 2.8 multiply_reduce_fusion.3
  63.7 1.6 fusion.24
  65.3 1.3 fusion.45
  66.7 3.4 fusion.17
  70.1 1.3 collective-permute-start.1
  71.4 1.0 fusion.40
  72.4 254.7 %psum.23 = f32[8]{0:T(128)S(1)} all-reduce(f32[8]{0:T(128)S(1)} %add.79), channel_id=1, replica_groups=mesh['group'=4,'dp'=32,'tensor'=4] {'group','dp'}, use_global_device_ids=true, to_apply=%region_15.16 | all-reduce | flops 8 | bytes 64 | tf_op jit(solution)/shard_map/psum | solution.py:155
  327.3 1.3 fusion.27
  328.8 0.9 pad_maximum_fusion.5
  330.2 2.3 fusion.28
  332.5 3.0 copy.96
  335.5 1.9 convert_element_type.156
  337.7 2.3 fusion.7
  340.1 1.2 multiply_convert_fusion
  341.9 0.9 add_bitcast_fusion
  342.8 2.6 multiply_reduce_fusion
  345.6 0.8 copy.178
  346.3 10.1 %psum.22 = f32[2,2,128]{2,1,0:T(2,128)S(1)} all-reduce(f32[2,2,128]{2,1,0:T(2,128)S(1)} %get-tuple-element.35), channel_id=1, replica_groups=mesh['group'=4,'dp'=32,'tensor'=4] {'tensor'}, use_global_device_ids=true, to_apply=%region_12.13 | all-reduce | flops 512 | bytes 4096 | tf_op jit(solution)/shard_map/psum | solution.py:152
  356.5 3.1 add_convert_fusion
  359.6 0.7 copy.103
  360.3 1.3 copy.177
  (88 shorter events, 5.1 us)
Async XLA Ops:
  0.6 18.0 %copy-start.10 = (bf16[128,1024]{1,0:T(8,128)(2,1)S(1)}, bf16[128,1024]{1,0:T(8,128)(2,1)}, u32[]{:S(2)}) copy-start(bf16[128,1024]{1,0:T(8,128)(2,1)} %param.10) | copy-start | bytes 786436
  18.7 2.1 copy-start.13
  21.4 1.0 copy-start.1
  21.5 1.0 copy-start.5
  22.4 2.6 copy-start.21
  22.4 2.6 copy-start.23
  24.9 1.0 copy-start.4
  24.9 4.4 %copy-start.15 = (s32[1,64]{1,0:T(1,128)S(1)}, s32[1,64]{1,0:T(1,128)}, u32[]{:S(2)}) copy-start(s32[1,64]{1,0:T(1,128)} %param.12) | copy-start | bytes 772
  24.9 6.8 %copy-start.9 = (bf16[128,1024]{1,0:T(8,128)(2,1)S(1)}, bf16[128,1024]{1,0:T(8,128)(2,1)}, u32[]{:S(2)}) copy-start(bf16[128,1024]{1,0:T(8,128)(2,1)} %param.9) | copy-start | bytes 786436
  25.0 6.9 %copy-start.8 = (bf16[128,1024]{1,0:T(8,128)(2,1)S(1)}, bf16[128,1024]{1,0:T(8,128)(2,1)}, u32[]{:S(2)}) copy-start(bf16[128,1024]{1,0:T(8,128)(2,1)} %param.15) | copy-start | bytes 786436
  26.3 8.2 %copy-start.17 = (f32[8]{0:T(128)S(1)}, f32[8]{0:T(128)}, u32[]{:S(2)}) copy-start(f32[8]{0:T(128)} %param.14) | copy-start | bytes 100
  27.2 31.4 %collective-permute-start = (bf16[256,8,128]{2,0,1:T(8,128)(2,1)}, bf16[256,8,128]{2,0,1:T(8,128)(2,1)}, u32[]{:S(2)}, u32[]{:S(2)}) collective-permute-start(bf16[256,8,128]{2,0,1:T(8,128)(2,1)} %copy.79), channel_id=1, source_target_pairs={{0,4},{4,8},{8,12},{12,16},{16,20},{20,24},{24,28},{28,32},{32,36}... | collective-permute-start | bytes 1572872 | tf_op jit(solution)/shard_map/ppermute | solution.py:17
  38.2 1.0 copy-start.3
  48.4 1.9 slice-start
  48.4 3.4 copy-start.7
  50.3 1.8 copy-start.12
  50.3 2.1 copy-start.20
  50.3 2.1 copy-start.14
  50.3 2.1 copy-start.16
  58.6 2.3 copy-start.11
  65.3 6.0 %copy-start.19 = (f32[8]{0:T(128)S(1)}, f32[8]{0:T(128)}, u32[]{:S(2)}) copy-start(f32[8]{0:T(128)} %get-tuple-element.17) | copy-start | bytes 100
  70.1 260.1 %collective-permute-start.1 = (bf16[256,8,128]{0,2,1:T(8,128)(2,1)}, bf16[256,8,128]{0,2,1:T(8,128)(2,1)S(1)}, u32[]{:S(2)}, u32[]{:S(2)}) collective-permute-start(bf16[256,8,128]{0,2,1:T(8,128)(2,1)} %fusion.17), channel_id=1, source_target_pairs={{4,0},{8,4},{12,8},{16,12},{20,16},{24,20},{28,24},{32,28},{36,32}... | collective-permute-start | bytes 1572872 | tf_op jit(solution)/shard_map/ppermute | solution.py:17
  71.4 258.3 %copy-start.18 = (f32[8]{0:T(128)S(1)}, f32[8]{0:T(128)}, u32[]{:S(2)}) copy-start(f32[8]{0:T(128)} %param.14) | copy-start | bytes 100
  335.5 2.2 copy-start
  335.5 4.6 %copy-start.22 = (f32[2,2,8,128,192]{3,4,2,1,0:T(8,128)S(1)}, f32[2,2,8,128,192]{3,4,2,1,0:T(8,128)}, u32[]{:S(2)}) copy-start(f32[2,2,8,128,192]{3,4,2,1,0:T(8,128)} %copy-done.21) | copy-start | bytes 9437188
  337.7 2.3 copy-start.2
  337.7 2.4 copy-start.6
  337.7 2.4 copy-start.24
where the time goes:
time: 362 us
  blocking collectives  278 us (77%)
  matrix products  36.8 us (10%)
  other arithmetic  22.9 us (6%)
  local copies, waits for them, and re-layouts  18.3 us (5%)
    psum x1, blocking collectives, shards(): summed = lax.psum(gate_terms, ('group', 'dp'))  255 us
    dot_general x18, matrix products, product(): return jnp.einsum(form, left, right, preferred_element_type=jnp.float32)  36.8 us
    psum x1, blocking collectives, shards(): square_sum = lax.psum(jnp.sum(floats * floats, axis=(3, 4)), 'tensor')  13.6 us
    psum x1, blocking collectives, shards(): lax.psum(jnp.sum(gain_grad * scaled, axis=(3, 4)), 'tensor') / full_width  10.1 us
    unnamed x66, local copies, waits for them, and re-layouts  8.57 us
  transfers between devices with their start and end apart: 2, of which 0 were waited for; matrix products, arithmetic and copies ran while one was open for 9% of the time, Pallas kernels for 0%

commit v1 on v0

--- a/solution.py
+++ b/solution.py
@@ -1,3 +1,4 @@
+import functools
 import math
 import jax
 import jax.numpy as jnp
@@ -9,6 +10,15 @@
 NL = 128
 epsilon = 1e-05
 masked_score = -1e30
+
+
+def fit_runs(arr_in, mesh_ax, device_axis):
+    for i0 in (mesh_ax, device_axis):
+        arr_in = lax.psum(arr_in, i0)
+    return arr_in
+
+
+attach_the_set = functools.partial(fit_runs, mesh_ax="group", device_axis="dp")
 
 
 def shifted(value, axis, steps):
@@ -152,7 +162,7 @@
     projection = lax.psum(jnp.sum(gain_grad * scaled, axis=(3, 4)), "tensor") / full_width
     neighbour_grad = grad_encoded + inverse * (gain_grad - scaled * projection[..., None, None])
     total_tokens = lax.axis_size("group") * lax.axis_size("dp") * row_count
-    summed = lax.psum(gate_terms, ("group", "dp"))
+    summed = attach_the_set(gate_terms)
     gate_grad = (1.0 - gate_tanh * gate_tanh) * summed / math.sqrt(total_tokens)
     return (
         cross_output,

time: 362 us -> 195 us (0.54)
  blocking collectives: 278 us -> 111 us
    psum x1 -> x2, blocking collectives: 255 us -> 87.1 us  [fit_runs(): arr_in = lax.psum(arr_in, i0)]
  transfers between devices with their start and end apart: 2 -> 2, of which waited for: 0 -> 0; matrix products, arithmetic and copies ran while one was open for 9% -> 16% of each run, Pallas kernels for 0% -> 0%
where the time goes in v1:
time: 195 us; the launch traced here: 194 us
  blocking collectives  111 us (57%)
  matrix products  36.8 us (19%)
  other arithmetic  22.9 us (12%)
  local copies, waits for them, and re-layouts  18.3 us (9%)
  starting transfers between devices  3.38 us (2%)
    psum x2, blocking collectives, fit_runs(): arr_in = lax.psum(arr_in, i0)  87.1 us
    dot_general x18, matrix products, product(): return jnp.einsum(form, left, right, preferred_element_type=jnp.float32)  36.8 us
    psum x1, blocking collectives, shards(): square_sum = lax.psum(jnp.sum(floats * floats, axis=(3, 4)), 'tensor')  13.6 us
    psum x1, blocking collectives, shards(): lax.psum(jnp.sum(gain_grad * scaled, axis=(3, 4)), 'tensor') / full_width  10.1 us
    unnamed x66, local copies, waits for them, and re-layouts  8.56 us
    unnamed x3, other arithmetic  4.53 us
  transfers between devices with their start and end apart: 2, of which 0 were waited for; matrix products, arithmetic and copies ran while one was open for 16% of the time, Pallas kernels for 0%

profile of v1, /device:TPU:2, one launch (start us, length us, event | category | flops | bytes accessed | tf_op | source)
XLA Modules:
  0.0 193.9 jit_solution(5156861810261073541)
XLA Ops:
  0.6 1.5 fusion.4
  2.2 2.8 %convert_bitcast_fusion = f32[64,8,8,128]{3,1,2,0:T(8,128)} fusion(bf16[512,1024]{1,0:T(8,128)(2,1)} %param.11), kind=kLoop, calls=%fused_computation.8 | loop fusion | flops 524288 | bytes 3145728
  5.0 13.6 %psum.28 = f32[2,2,128]{2,1,0:T(2,128)S(1)} all-reduce(f32[2,2,128]{2,1,0:T(2,128)S(1)} %bitcast.184), channel_id=1, replica_groups=mesh['group'=4,'dp'=32,'tensor'=4] {'tensor'}, use_global_device_ids=true, to_apply=%region_1.0 | all-reduce | flops 512 | bytes 4096 | tf_op jit(solution)/shard_map/psum | solution.py:107
  18.7 2.1 %copy.109 = f32[64,8,8,128]{3,2,1,0:T(8,128)S(1)} copy(f32[64,8,8,128]{3,1,2,0:T(8,128)} %convert_bitcast_fusion) | data formatting | bytes 4194304
  21.5 0.8 fusion.3
  22.5 2.4 %fusion.6 = (bf16[2,2,128,8,128]{4,2,3,1,0:T(8,128)(2,1)S(1)}, f32[2,2,8,128,128]{3,4,2,1,0:T(8,128)}) fusion(f32[2,2,128,8,128]{4,3,2,1,0:T(8,128)S(1)} %bitcast.148, f32[2,2,8,128]{3,2,1,0:T(8,128)S(1)} %get-tuple-element.26, f32[2,2,8,128,192]{3,4,2,1,0:T(8,128)S(1)} %get-tuple-element.27, bf16[2,2,64,8,128]{4,2,3,1,0:T(8,128)(2,1)S(1)} %broadcast_in_dim.103, ...), kind=kOutput, calls=%fused_computation.14 | convolution fusion | flops 207880192 | bytes 9977856 | tf_op jit(solution)/shard_map/cjhqk,cjkhd->cjqhd/dot_general | solution.py:31
  25.0 0.9 copy-done.4
  26.3 0.9 copy.79
  27.2 2.1 %collective-permute-start = (bf16[256,8,128]{2,0,1:T(8,128)(2,1)}, bf16[256,8,128]{2,0,1:T(8,128)(2,1)}, u32[]{:S(2)}, u32[]{:S(2)}) collective-permute-start(bf16[256,8,128]{2,0,1:T(8,128)(2,1)} %copy.79), channel_id=1, source_target_pairs={{0,4},{4,8},{8,12},{12,16},{16,20},{20,24},{24,28},{28,32},{32,36}... | collective-permute-start | bytes 1572872 | tf_op jit(solution)/shard_map/ppermute | solution.py:27
  30.5 1.2 iota_compare_fusion.1
  31.8 0.7 slice.76
  32.5 1.9 copy.82
  35.0 0.6 broadcast_compare_fusion
  35.8 0.9 convert_bitcast_fusion.1
  36.8 0.9 copy.117
  38.2 1.0 copy-done.3
  39.2 1.2 fusion.66
  40.4 5.0 %multiply_reduce_fusion.1 = (f32[8]{0:T(128)}, f32[2,64,8]{1,2,0:T(8,128)}, bf16[2,64,8,128]{3,1,2,0:T(8,128)(2,1)}) fusion(f32[2,64,8,128]{3,2,1,0:T(8,128)} %bitcast.171, f32[8]{0:T(128)} %tanh.3, pred[2]{0:T(512)(128)(4,1)} %get-tuple-element.21, bf16[2,256,8,128]{3,2,1,0:T(8,128)(2,1)S(1)} %bitcast.155, f32[2,8,64]{2,1,0:T(8,128)S(1)} %get-tuple-element.30, ...), kind=kOutput, calls=%fused_computation.63 | convolution fusion | flops 69075192 | bytes 2891842 | tf_op jit(solution)/shard_map/bhrm,bmhd->brhd/dot_general | solution.py:31
  45.4 2.0 %fusion.13 = bf16[2,8,64,256]{3,2,1,0:T(8,128)(2,1)S(1)} fusion(bf16[2,256,8,128]{3,2,1,0:T(8,128)(2,1)S(1)} %bitcast.156, f32[2,8,64]{2,1,0:T(8,128)} %bitcast.186, f32[2,8,64,256]{3,2,1,0:T(8,128)} %get-tuple-element.31, f32[2,8,64]{2,1,0:T(8,128)S(1)} %get-tuple-element.30, f32[2,64,8,128]{3,2,1,0:T(8,128)} %bitcast.172, f32[8]{0:T(128)} %tanh.3, ...), kind=kOutput, calls=%fused_computation.30 | convolution fusion | flops 68812800 | bytes 3153954 | tf_op jit(solution)/shard_map/brhd,bmhd->bhrm/dot_general | solution.py:31
  47.4 1.0 fusion.26
  48.4 1.9 fusion.41
  50.3 0.8 convert_bitcast_fusion.3
  51.1 0.8 copy.115
  52.5 6.2 %add_bitcast_fusion.1 = f32[2,256,8,128]{1,3,2,0:T(8,128)} fusion(f32[2,8,128,256]{3,2,1,0:T(8,128)} %fusion.41, f32[2,64,8,128]{3,2,1,0:T(8,128)} %bitcast.173, f32[8]{0:T(128)S(1)} %copy-done.14, pred[2]{0:T(512)(128)(4,1)S(1)} %copy-done.16, f32[2,8,64]{2,1,0:T(8,128)S(1)} %get-tuple-element.30, f32[2,8,64,256]{3,2,1,0:T(8,128)} %copy-done.3), kind=kOutput, calls=%fused_computation.18 | convolution fusion | flops 68814080 | bytes 5771298 | tf_op jit(solution)/shard_map/bhrm,brhd->bmhd/dot_general | solution.py:31
  58.6 1.4 fusion.21
  60.0 0.9 fusion.67
  60.9 2.8 %multiply_reduce_fusion.3 = (f32[8]{0:T(128)S(1)}, f32[64,8]{0,1:T(8,128)S(1)}, f32[1,64,8,128]{3,1,2,0:T(8,128)}) fusion(f32[1,64,8,128]{3,2,1,0:T(8,128)S(1)} %bitcast.179, f32[8]{0:T(128)S(1)} %copy-done.14, pred[]{:T(512)S(6)} %and.13, bf16[256,8,128]{2,0,1:T(8,128)(2,1)} %collective-permute-done, f32[8,64]{1,0:T(8,128)S(1)} %get-tuple-element.32, ...), kind=kOutput, calls=%fused_computation.82 | convolution fusion | flops 34406648 | bytes 1577025 | tf_op jit(solution)/shard_map/bhrm,bmhd->brhd/dot_general | solution.py:31
  63.7 1.6 fusion.24
  65.3 1.3 fusion.45
  66.7 3.4 %fusion.17 = bf16[256,8,128]{0,2,1:T(8,128)(2,1)} fusion(f32[8,128,256]{2,1,0:T(8,128)} %fusion.45, f32[8,8,8,128]{3,2,1,0:T(8,128)} %get-tuple-element.24, f32[8]{0:T(128)S(1)} %copy-done.14, pred[]{:T(512)S(6)} %and.13, f32[8,64]{1,0:T(8,128)S(1)} %get-tuple-element.32, f32[8,64,256]{2,1,0:T(8,128)S(1)} %fusion.21), kind=kOutput, calls=%fused_computation.34 | convolution fusion | flops 34669312 | bytes 2361377 | tf_op jit(solution)/shard_map/bhrm,brhd->bmhd/dot_general | solution.py:31
  70.1 1.3 collective-permute-start.1
  71.4 16.4 %psum.30 = f32[8]{0:T(128)S(1)} all-reduce(f32[8]{0:T(128)S(1)} %add.81), channel_id=1, replica_groups=mesh['group'=4,'dp'=32,'tensor'=4] {'group'}, use_global_device_ids=true, to_apply=%region_15.16 | all-reduce | flops 8 | bytes 64 | tf_op jit(solution)/shard_map/psum | solution.py:17
  87.7 1.1 fusion.40
  88.8 70.7 %psum.31 = f32[8]{0:T(128)S(1)} all-reduce(f32[8]{0:T(128)S(1)} %psum.30), channel_id=1, replica_groups=mesh['group'=4,'dp'=32,'tensor'=4] {'dp'}, use_global_device_ids=true, to_apply=%region_16.17 | all-reduce | flops 8 | bytes 64 | tf_op jit(solution)/shard_map/psum | solution.py:17
  159.6 1.3 fusion.27
  161.1 0.9 pad_maximum_fusion.5
  162.5 2.3 %fusion.28 = f32[2,256,8,128]{1,3,2,0:T(8,128)} fusion(f32[2,256,8,128]{1,3,2,0:T(8,128)} %add_bitcast_fusion.1, bf16[256,8,128]{0,2,1:T(8,128)(2,1)S(1)} %collective-permute-done.1), kind=kLoop, calls=%fused_computation.54 | loop fusion | flops 524288 | bytes 2621440 | tf_op jit(solution)/shard_map/scatter-add | solution.py:146
  164.9 3.0 %copy.96 = f32[2,256,8,128]{3,2,1,0:T(8,128)} copy(f32[2,256,8,128]{1,3,2,0:T(8,128)} %fusion.28) | data formatting | bytes 4194304 | tf_op jit(solution)/shard_map/scatter-add | solution.py:146
  167.9 1.9 convert_element_type.156
  170.1 2.3 %fusion.7 = f32[2,2,128,8]{2,3,1,0:T(8,128)S(1)} fusion(f32[2,2,8,128,128]{3,4,2,1,0:T(8,128)} %get-tuple-element.29, f32[2,2,128,8,128]{4,3,2,1,0:T(8,128)S(1)} %bitcast.153), kind=kLoop, calls=%fused_computation.15 | loop fusion | flops 1044480 | bytes 4210688 | tf_op jit(solution)/shard_map/reduce_sum | solution.py:53
  172.5 1.2 multiply_convert_fusion
  174.2 0.9 add_bitcast_fusion
  175.1 2.6 %multiply_reduce_fusion = (f32[2,2,128]{2,1,0:T(2,128)S(1)}, f32[2,2,128,8,128]{4,2,3,1,0:T(8,128)}) fusion(f32[2,2,128,8,128]{4,3,2,1,0:T(8,128)S(1)} %bitcast.149, f32[2,2,128]{2,1,0:T(2,128)S(1)} %add_rsqrt_fusion, f32[8,128]{1,0:T(8,128)S(1)} %bitcast.182, f32[2,2,192,8,128]{4,2,3,1,0:T(8,128)S(1)} %add_bitcast_fusion, ...), kind=kOutput, calls=%fused_computation.17 | convolution fusion | flops 207093248 | bytes 9445376 | tf_op jit(solution)/shard_map/cjhqk,cjkhd->cjqhd/dot_general | solution.py:31
  177.9 0.8 copy.178
  178.7 10.1 %psum.29 = f32[2,2,128]{2,1,0:T(2,128)S(1)} all-reduce(f32[2,2,128]{2,1,0:T(2,128)S(1)} %get-tuple-element.35), channel_id=1, replica_groups=mesh['group'=4,'dp'=32,'tensor'=4] {'tensor'}, use_global_device_ids=true, to_apply=%region_12.13 | all-reduce | flops 512 | bytes 4096 | tf_op jit(solution)/shard_map/psum | solution.py:162
  188.8 3.1 %add_convert_fusion = bf16[2,2,128,8,128]{4,2,3,1,0:T(8,128)(2,1)S(1)} fusion(f32[2,2,128,8,128]{4,2,3,1,0:T(8,128)} %get-tuple-element.36, f32[2,2,128,8,128]{4,3,2,1,0:T(8,128)} %bitcast.152, f32[2,2,128,8,128]{4,3,2,1,0:T(8,128)S(1)} %bitcast.150, f32[2,2,128]{2,1,0:T(2,128)S(1)} %broadcast_multiply_fusion, f32[2,2,128]{2,1,0:T(2,128)S(1)} %add_rsqrt_fusion), kind=kLoop, calls=%fused_computation.16 | loop fusion | flops 3145728 | bytes 7344128 | tf_op jit(solution)/shard_map/convert_element_type | solution.py:171
  191.9 0.7 copy.103
  192.6 1.3 copy.177
  (89 shorter events, 5.7 us)
Async XLA Ops:
  0.6 18.0 %copy-start.10 = (bf16[128,1024]{1,0:T(8,128)(2,1)S(1)}, bf16[128,1024]{1,0:T(8,128)(2,1)}, u32[]{:S(2)}) copy-start(bf16[128,1024]{1,0:T(8,128)(2,1)} %param.10) | copy-start | bytes 786436
  18.7 2.1 %copy-start.13 = (f32[1024]{0:T(1024)S(1)}, f32[1024]{0:T(1024)}, u32[]{:S(2)}) copy-start(f32[1024]{0:T(1024)} %param.13) | copy-start | bytes 12292
  21.4 1.0 copy-start.1
  21.5 1.0 copy-start.5
  22.4 2.6 %copy-start.21 = (f32[2,2,8,128,192]{3,4,2,1,0:T(8,128)}, f32[2,2,8,128,192]{3,4,2,1,0:T(8,128)S(1)}, u32[]{:S(2)}) copy-start(f32[2,2,8,128,192]{3,4,2,1,0:T(8,128)S(1)} %get-tuple-element.27) | copy-start | bytes 9437188
  22.4 2.6 %copy-start.23 = (f32[2,2,8,128]{3,2,1,0:T(8,128)}, f32[2,2,8,128]{3,2,1,0:T(8,128)S(1)}, u32[]{:S(2)}) copy-start(f32[2,2,8,128]{3,2,1,0:T(8,128)S(1)} %get-tuple-element.26) | copy-start | bytes 49156
  24.9 1.0 copy-start.4
  24.9 4.4 %copy-start.15 = (s32[1,64]{1,0:T(1,128)S(1)}, s32[1,64]{1,0:T(1,128)}, u32[]{:S(2)}) copy-start(s32[1,64]{1,0:T(1,128)} %param.12) | copy-start | bytes 772
  24.9 6.8 %copy-start.9 = (bf16[128,1024]{1,0:T(8,128)(2,1)S(1)}, bf16[128,1024]{1,0:T(8,128)(2,1)}, u32[]{:S(2)}) copy-start(bf16[128,1024]{1,0:T(8,128)(2,1)} %param.9) | copy-start | bytes 786436
  25.0 6.9 %copy-start.8 = (bf16[128,1024]{1,0:T(8,128)(2,1)S(1)}, bf16[128,1024]{1,0:T(8,128)(2,1)}, u32[]{:S(2)}) copy-start(bf16[128,1024]{1,0:T(8,128)(2,1)} %param.15) | copy-start | bytes 786436
  26.3 8.2 %copy-start.17 = (f32[8]{0:T(128)S(1)}, f32[8]{0:T(128)}, u32[]{:S(2)}) copy-start(f32[8]{0:T(128)} %param.14) | copy-start | bytes 100
  27.2 31.4 %collective-permute-start = (bf16[256,8,128]{2,0,1:T(8,128)(2,1)}, bf16[256,8,128]{2,0,1:T(8,128)(2,1)}, u32[]{:S(2)}, u32[]{:S(2)}) collective-permute-start(bf16[256,8,128]{2,0,1:T(8,128)(2,1)} %copy.79), channel_id=1, source_target_pairs={{0,4},{4,8},{8,12},{12,16},{16,20},{20,24},{24,28},{28,32},{32,36}... | collective-permute-start | bytes 1572872 | tf_op jit(solution)/shard_map/ppermute | solution.py:27
  38.2 1.0 copy-start.3
  48.4 1.9 slice-start
  48.4 3.4 %copy-start.7 = (bf16[2,64,8,128]{3,1,2,0:T(8,128)(2,1)S(1)}, bf16[2,64,8,128]{3,1,2,0:T(8,128)(2,1)}, u32[]{:S(2)}) copy-start(bf16[2,64,8,128]{3,1,2,0:T(8,128)(2,1)} %fusion.26) | copy-start | bytes 786436
  50.3 1.8 copy-start.12
  50.3 2.1 %copy-start.20 = (pred[2]{0:T(512)(128)(4,1)S(1)}, pred[2]{0:T(512)(128)(4,1)}, u32[]{:S(2)}) copy-start(pred[2]{0:T(512)(128)(4,1)} %iota_compare_fusion.1) | copy-start | bytes 10
  50.3 2.1 %copy-start.14 = (f32[8]{0:T(128)S(1)}, f32[8]{0:T(128)}, u32[]{:S(2)}) copy-start(f32[8]{0:T(128)} %tanh.3) | copy-start | bytes 100
  50.3 2.1 %copy-start.16 = (pred[2]{0:T(512)(128)(4,1)S(1)}, pred[2]{0:T(512)(128)(4,1)}, u32[]{:S(2)}) copy-start(pred[2]{0:T(512)(128)(4,1)} %get-tuple-element.21) | copy-start | bytes 10
  58.6 2.3 %copy-start.11 = (f32[8,8,8,128]{3,2,1,0:T(8,128)S(1)}, f32[8,8,8,128]{3,2,1,0:T(8,128)}, u32[]{:S(2)}) copy-start(f32[8,8,8,128]{3,2,1,0:T(8,128)} %copy.115) | copy-start | bytes 786436
  65.3 4.7 %copy-start.19 = (f32[8]{0:T(128)S(1)}, f32[8]{0:T(128)}, u32[]{:S(2)}) copy-start(f32[8]{0:T(128)} %get-tuple-element.17) | copy-start | bytes 100
  70.1 92.5 %collective-permute-start.1 = (bf16[256,8,128]{0,2,1:T(8,128)(2,1)}, bf16[256,8,128]{0,2,1:T(8,128)(2,1)S(1)}, u32[]{:S(2)}, u32[]{:S(2)}) collective-permute-start(bf16[256,8,128]{0,2,1:T(8,128)(2,1)} %fusion.17), channel_id=1, source_target_pairs={{4,0},{8,4},{12,8},{16,12},{20,16},{24,20},{28,24},{32,28},{36,32}... | collective-permute-start | bytes 1572872 | tf_op jit(solution)/shard_map/ppermute | solution.py:27
  87.7 74.3 %copy-start.18 = (f32[8]{0:T(128)S(1)}, f32[8]{0:T(128)}, u32[]{:S(2)}) copy-start(f32[8]{0:T(128)} %param.14) | copy-start | bytes 100
  167.9 2.2 %copy-start = (f32[2,256,8,128]{3,2,1,0:T(8,128)S(1)}, f32[2,256,8,128]{3,2,1,0:T(8,128)}, u32[]{:S(2)}) copy-start(f32[2,256,8,128]{3,2,1,0:T(8,128)} %copy.96) | copy-start | bytes 6291460
  167.9 4.6 %copy-start.22 = (f32[2,2,8,128,192]{3,4,2,1,0:T(8,128)S(1)}, f32[2,2,8,128,192]{3,4,2,1,0:T(8,128)}, u32[]{:S(2)}) copy-start(f32[2,2,8,128,192]{3,4,2,1,0:T(8,128)} %copy-done.21) | copy-start | bytes 9437188
  170.1 2.3 %copy-start.2 = (bf16[2,2,128,8,128]{4,2,3,1,0:T(8,128)(2,1)S(1)}, bf16[2,2,128,8,128]{4,2,3,1,0:T(8,128)(2,1)}, u32[]{:S(2)}) copy-start(bf16[2,2,128,8,128]{4,2,3,1,0:T(8,128)(2,1)} %copy-done.1) | copy-start | bytes 3145732
  170.1 2.4 %copy-start.6 = (bf16[2,2,64,8,128]{4,2,3,1,0:T(8,128)(2,1)S(1)}, bf16[2,2,64,8,128]{4,2,3,1,0:T(8,128)(2,1)}, u32[]{:S(2)}) copy-start(bf16[2,2,64,8,128]{4,2,3,1,0:T(8,128)(2,1)} %copy-done.5) | copy-start | bytes 1572868
  170.1 2.4 %copy-start.24 = (f32[2,2,8,128]{3,2,1,0:T(8,128)S(1)}, f32[2,2,8,128]{3,2,1,0:T(8,128)}, u32[]{:S(2)}) copy-start(f32[2,2,8,128]{3,2,1,0:T(8,128)} %copy-done.23) | copy-start | bytes 49156
